TPU v7x, 256 devices: a whole 4x4x8 slice. The times are simulated.
256 devices in a mesh: dp: 16 (over y, z_hi, core), fsdp: 16 (over z_lo, x).
Axes of the slice: x: 4, y: 4, z: 8 (z_hi: 2, z_lo: 4; z = z_hi * 4 + z_lo), core: 2. Of those that a mesh axis runs over, the one named last changes fastest.
Arguments:
- tokens: bfloat16 [8192, 5120], P('dp', 'fsdp'), may hold values from -6 to 6
- norm_gain: float32 [5120], replicated, may hold values from 0.25 to 1.75
- expansion: bfloat16 [5120, 4096], P(None, 'fsdp'), may hold values from -0.078125 to 0.078125
- small_weight: bfloat16 [4096, 4096], P(None, 'fsdp'), may hold values from -0.09375 to 0.09375
- cotangent: bfloat16 [8192, 5120], P('dp', 'fsdp'), may hold values from -6 to 6
Outputs:
- mixed: bfloat16 [8192, 5120], P('dp', 'fsdp')
- operator_grad: float32 [5120, 4096], P(None, 'fsdp')
All inputs are finite; a program needn't handle non-finite values.
Results may differ from a plain program's by a relative error of at most 0.0058.
Values may be sent and summed in bfloat16 or wider, within the bound.
A program may use at most 128 MiB of HBM per device.

v0:
```python
import jax
import jax.numpy as jnp
from jax import lax
from jax.sharding import PartitionSpec as P


def transpose_dot(left, right):
    return lax.dot_general(
        left, right, (((0,), (0,)), ((), ())), preferred_element_type=jnp.float32
    )


def per_device(tokens, norm_gain, expansion, small_weight, cotangent):
    whole, whole_back = (
        lax.all_gather(tokens, "fsdp", axis=1, tiled=True),
        lax.all_gather(cotangent, "fsdp", axis=1, tiled=True),
    )
    wide = whole.astype(jnp.float32)
    scale = lax.rsqrt(jnp.mean(wide * wide, axis=1, keepdims=True) + 1e-05)
    normed = (wide * scale * norm_gain[None, :]).astype(jnp.bfloat16)
    reduced = jnp.dot(normed, expansion, preferred_element_type=jnp.float32).astype(jnp.bfloat16)
    partial_mix = jnp.dot(reduced, small_weight.T, preferred_element_type=jnp.float32)
    projected = lax.psum_scatter(partial_mix, "fsdp", scatter_dimension=1, tiled=True).astype(
        jnp.bfloat16
    )
    partial_out = jnp.dot(projected, expansion.T, preferred_element_type=jnp.float32)
    branch = lax.psum_scatter(partial_out, "fsdp", scatter_dimension=1, tiled=True)
    mixed = (tokens.astype(jnp.float32) + branch).astype(jnp.bfloat16)
    back_small = jnp.dot(whole_back, expansion, preferred_element_type=jnp.float32).astype(
        jnp.bfloat16
    )
    back_full = lax.all_gather(back_small, "fsdp", axis=1, tiled=True)
    back_reduced = jnp.dot(back_full, small_weight, preferred_element_type=jnp.float32).astype(
        jnp.bfloat16
    )
    grad = transpose_dot(whole_back, projected) + transpose_dot(normed, back_reduced)
    grad = lax.psum(grad, "dp")
    return (mixed, grad)


def solution(mesh):
    in_specs = (P("dp", "fsdp"), P(), P(None, "fsdp"), P(None, "fsdp"), P("dp", "fsdp"))
    out_specs = (P("dp", "fsdp"), P(None, "fsdp"))
    return jax.shard_map(
        per_device, mesh=mesh, in_specs=in_specs, out_specs=out_specs, check_vma=False
    )
```

profile of v0, /device:TPU:1, one launch (start us, length us, event | category | flops | bytes accessed | tf_op | source)
XLA Modules:
  0.0 788.9 jit_solution(2901583038899941567)
XLA Ops:
  7.2 0.0 copy-start
  7.2 0.0 all-gather.6.cloned.1.call-start
  7.2 0.7 all-gather.6.cloned.1.call-update
  7.9 0.0 all-gather.4.cloned.1.call-start
  8.0 0.7 all-gather.4.cloned.1.call-update
  8.7 0.0 all-gather.8.cloned.1.call-start
  8.7 87.2 %all-gather.6.cloned.1.call-done = bf16[512,5120]{0,1:T(8,128)(2,1)} async-done(((bf16[512,320]{0,1:T(8,128)(2,1)}), bf16[512,5120]{0,1:T(8,128)(2,1)}) %all-gather.6.cloned.1.call-update) | async-done | bytes 5242896 | tf_op jit(solution)/shard_map/all_gather | solution.py:16
  95.9 0.0 copy-done
  95.9 4.8 convolution_convert_fusion.1
  100.7 0.0 all-gather.8.cloned.1.call-update
  100.7 0.0 reduce-scatter.3.cloned.1.call-start
  100.8 85.1 %all-gather.4.cloned.1.call-done = bf16[512,5120]{0,1:T(8,128)(2,1)} async-done(((bf16[512,320]{0,1:T(8,128)(2,1)}), bf16[512,5120]{0,1:T(8,128)(2,1)}) %all-gather.4.cloned.1.call-update) | async-done | bytes 5242896 | tf_op jit(solution)/shard_map/all_gather | solution.py:15
  185.9 3.6 fusion
  189.5 0.0 copy-done.3
  189.5 11.5 %fusion.12 = f32[512,4096]{1,0:T(8,128)} fusion(bf16[4096,256]{1,0:T(8,128)(2,1)} %param.8, bf16[5120,256]{1,0:T(8,128)(2,1)S(1)} %copy-done, bf16[512,5120]{0,1:T(8,128)(2,1)} %all-gather.4.cloned.1.call-done, f32[5120]{0:T(1024)S(1)} %copy-done.3, f32[512]{0:T(512)S(1)} %add_rsqrt_fusion), kind=kOutput, calls=%fused_computation.10 | convolution fusion | flops 2426535936 | bytes 18372608 | tf_op jit(solution)/shard_map/dot_general | solution.py:22
  201.0 0.0 reduce-scatter.3.cloned.1.call-update
  201.0 0.2 all-reduce.2.cloned.1.call-start
  201.3 73.2 %all-gather.8.cloned.1.call-done = bf16[512,4096]{1,0:T(8,128)(2,1)} async-done(((bf16[512,256]{1,0:T(8,128)(2,1)}), bf16[512,4096]{1,0:T(8,128)(2,1)}) %all-gather.8.cloned.1.call-update) | async-done | bytes 4194320 | tf_op jit(solution)/shard_map/all_gather | solution.py:32
  274.5 11.6 %fusion.4 = f32[5120,256]{0,1:T(8,128)} fusion(bf16[512,5120]{0,1:T(8,128)(2,1)} %all-gather.4.cloned.1.call-done, f32[5120]{0:T(1024)S(1)} %copy-done.3, f32[512]{0:T(512)S(1)} %add_rsqrt_fusion, bf16[512,4096]{1,0:T(8,128)(2,1)} %all-gather.8.cloned.1.call-done, bf16[4096,256]{1,0:T(8,128)(2,1)} %param.8), kind=kOutput, calls=%fused_computation.7 | convolution fusion | flops 2426535936 | bytes 16799744 | tf_op jit(solution)/shard_map/dot_general | solution.py:8
  286.1 100.4 %reduce-scatter.3.cloned.1.call-done = f32[512,256]{1,0:T(8,128)} async-done(((f32[512,4096]{1,0:T(8,128)}), f32[512,256]{1,0:T(8,128)}) %reduce-scatter.3.cloned.1.call-update) | async-done | bytes 524304 | tf_op jit(solution)/shard_map/reduce_scatter | solution.py:23
  386.4 8.2 %fusion.3 = f32[5120,256]{0,1:T(8,128)} fusion(f32[5120,256]{0,1:T(8,128)} %fusion.4, bf16[512,5120]{0,1:T(8,128)(2,1)} %all-gather.6.cloned.1.call-done, f32[512,256]{1,0:T(8,128)} %reduce-scatter.3.cloned.1.call-done), kind=kOutput, calls=%fused_computation.6 | convolution fusion | flops 1343619072 | bytes 16252928 | tf_op jit(solution)/shard_map/dot_general | solution.py:8
  394.6 0.0 all-reduce.2.cloned.1.call-update
  394.6 0.0 reduce-scatter.5.cloned.1.call-start
  394.7 1.0 copy-done.1
  395.6 5.5 fusion.15
  401.2 0.0 reduce-scatter.5.cloned.1.call-update
  401.2 0.0 copy-start.2
  401.2 250.5 %all-reduce.2.cloned.1.call-done = f32[5120,256]{0,1:T(8,128)} async-done(((f32[5120,256]{0,1:T(8,128)}), f32[5120,256]{0,1:T(8,128)}) %all-reduce.2.cloned.1.call-update) | async-done | bytes 5242896 | tf_op jit(solution)/shard_map/psum | solution.py:37
  651.6 5.9 copy.8
  657.5 122.6 %reduce-scatter.5.cloned.1.call-done = f32[512,320]{0,1:T(8,128)} async-done(((f32[512,5120]{0,1:T(8,128)}), f32[512,320]{0,1:T(8,128)}) %reduce-scatter.5.cloned.1.call-update) | async-done | bytes 655376 | tf_op jit(solution)/shard_map/reduce_scatter | solution.py:27
  780.1 0.0 copy-done.2
  780.1 1.9 add_convert_fusion
  (3 shorter events, 0.0 us)
Async XLA Ops:
  7.2 88.8 %copy-start = (bf16[5120,256]{1,0:T(8,128)(2,1)S(1)}, bf16[5120,256]{1,0:T(8,128)(2,1)}, u32[]{:S(2)}) copy-start(bf16[5120,256]{1,0:T(8,128)(2,1)} %param.7) | copy-start | bytes 7864324
  7.2 88.8 %all-gather.6.cloned.1.call-start = ((), (), s32[]{:S(2)}) async-start(), calls=%async_computation.5 | async-start | bytes 5570560 | tf_op jit(solution)/shard_map/all_gather | solution.py:16
  7.9 178.0 %all-gather.4.cloned.1.call-start = ((), (), s32[]{:S(2)}) async-start(), calls=%async_computation.2 | async-start | bytes 5570560 | tf_op jit(solution)/shard_map/all_gather | solution.py:15
  8.7 265.8 %all-gather.8.cloned.1.call-start = ((), (), s32[]{:S(2)}) async-start(), calls=%async_computation.6 | async-start | bytes 4456448 | tf_op jit(solution)/shard_map/all_gather | solution.py:32
  100.7 88.8 %copy-start.3 = (f32[5120]{0:T(1024)S(1)}, f32[5120]{0:T(1024)}, u32[]{:S(2)}) copy-start(f32[5120]{0:T(1024)} %param.6) | copy-start | bytes 61444
  100.7 285.7 %reduce-scatter.3.cloned.1.call-start = ((), (), s32[]{:S(2)}) async-start(), calls=%async_computation.3 | async-start | bytes 8912896 | tf_op jit(solution)/shard_map/reduce_scatter | solution.py:23
  201.0 450.6 %all-reduce.2.cloned.1.call-start = ((), (), s32[]{:S(2)}) async-start(), calls=%async_computation.7 | async-start | bytes 10485760 | tf_op jit(solution)/shard_map/psum | solution.py:37
  394.6 1.0 copy-start.1
  394.6 385.5 %reduce-scatter.5.cloned.1.call-start = ((), (), s32[]{:S(2)}) async-start(), calls=%async_computation.4 | async-start | bytes 11141120 | tf_op jit(solution)/shard_map/reduce_scatter | solution.py:27
  401.2 379.0 %copy-start.2 = (bf16[512,320]{0,1:T(8,128)(2,1)S(1)}, bf16[512,320]{0,1:T(8,128)(2,1)}, u32[]{:S(2)}) copy-start(bf16[512,320]{0,1:T(8,128)(2,1)} %param.5) | copy-start | bytes 983044
Sparse Core Ops, SparseCore 0:
  9.8 86.0 all-gather.5
  97.7 88.1 all-gather.3
  188.2 86.2 all-gather.7
  276.9 109.4 reduce-scatter.2
  394.7 256.8 all-reduce.1
  654.1 126.0 reduce-scatter.4
where the time goes:
time: 789 us
  waiting for transfers between devices  720 us (91%)
  matrix products  41.5 us (5%)
  between operations  14.1 us (2%)
    psum x1, waiting for transfers between devices, per_device(): grad = lax.psum(grad, 'dp')  250 us
    reduce_scatter x1, waiting for transfers between devices, per_device(): lax.psum_scatter(partial_out, 'fsdp', scatter_dimension=1, tiled=True)  123 us
    reduce_scatter x1, waiting for transfers between devices, per_device(): lax.psum_scatter(partial_mix, 'fsdp', scatter_dimension=1, tiled=True)  100 us
    all_gather x1, waiting for transfers between devices, per_device(): lax.all_gather(cotangent, 'fsdp', axis=1, tiled=True)  87.2 us
    all_gather x1, waiting for transfers between devices, per_device(): lax.all_gather(tokens, 'fsdp', axis=1, tiled=True)  85.1 us
    all_gather x1, waiting for transfers between devices, per_device(): back_full = lax.all_gather(back_small, 'fsdp', axis=1, tiled=True)  73.2 us
    dot_general x2, matrix products, transpose_dot(): lax.dot_general(left, right, (((0,), (0,)), ((), ())), preferred_element_...  19.7 us
  transfers between devices with their start and end apart: 6, of which 6 were waited for; matrix products, arithmetic and copies ran while one was open for 5% of the time, Pallas kernels for 0%

commit v1 on v0

v1 whole, which is shorter than its diff:
```python
import jax
import jax.numpy as jnp
from jax import lax
from jax.experimental import pallas as pl
from jax.experimental.pallas import tpu as pltpu
from jax.sharding import PartitionSpec as P

MESH = pl.DeviceIdType.MESH
F32 = jnp.float32
BF16 = jnp.bfloat16
N_SEMS = 160


def nn(a, b):
    return lax.dot_general(a, b, (((1,), (0,)), ((), ())), preferred_element_type=F32)


def nt(a, b):
    return lax.dot_general(a, b, (((1,), (1,)), ((), ())), preferred_element_type=F32)


def kernel(
    x_ref, gain_ref, e_ref, w_ref, c_ref, mixed_ref, fg,
    stat_x, stat_z, gx, gc, normed, eb, ebt, wb, wbt,
    r_s, r_r, r_g, p_s, p_r, p_g, b_s, b_r, b_g, q_s, q_r, q_g,
    o_s, o_r, acc, o_own, grad, gs, gr, ys, yr, zs, zr, y_own, z_own, x_s,
    ss, rs, ls,
):
    chunk, tok = x_ref.shape
    sub = w_ref.shape[2]
    features = chunk * 16
    d, f = lax.axis_index("dp"), lax.axis_index("fsdp")
    y, h, c = d // 4, (d // 2) % 2, d % 2
    z, x = f // 4, f % 4

    def dev(y=y, h=h, c=c, z=z, x=x):
        return {"dp": y * 4 + h * 2 + c, "fsdp": z * 4 + x}

    def turn(v, k):
        return lax.rem(v + k + 4, 4)

    xp = [dev(x=turn(x, k)) for k in range(4)]
    zp = [dev(z=turn(z, k)) for k in range(4)]
    yp = [dev(y=turn(y, k)) for k in range(4)]
    hp, cp = dev(h=1 - h), dev(c=1 - c)
    right, left = dev(z=jnp.minimum(z + 1, 3)), dev(z=jnp.maximum(z - 1, 0))

    barrier = pltpu.get_barrier_semaphore()
    friends = xp[1:] + zp[1:] + yp[1:] + [hp, cp]
    for friend in friends:
        pl.semaphore_signal(barrier, inc=1, device_id=friend, device_id_type=MESH)
    pl.semaphore_wait(barrier, len(friends))

    counter = [0]
    pending = []

    def take(n):
        at = counter[0]
        counter[0] += n
        assert counter[0] <= N_SEMS
        return at

    def remote(src, dst, sem, to):
        return pltpu.make_async_remote_copy(
            src_ref=src, dst_ref=dst, send_sem=ss.at[sem], recv_sem=rs.at[sem],
            device_id=to, device_id_type=MESH,
        )

    def send(src, dst, sem, to):
        copy = remote(src, dst, sem, to)
        copy.start()
        pending.append(copy)
        return copy

    class Line:
        def __init__(self, own, slots):
            self.own, self.slots, self.sem = own, slots, take(8)

        def hop(self, s, way, own=False):
            src = self.own if own else self.slots.at[s]
            return pltpu.make_async_remote_copy(
                src_ref=src, dst_ref=self.slots.at[s],
                send_sem=ss.at[self.sem + 4 * way + s], recv_sem=rs.at[self.sem + s],
                device_id=left if way else right, device_id_type=MESH,
            )

        def begin(self):
            @pl.when(z < 3)
            def _():
                self.hop(z, 0, True).start()

            @pl.when(z > 0)
            def _():
                self.hop(z, 1, True).start()

        def step(self, distance):
            @pl.when(z - distance >= 0)
            def _():
                self.hop(z - distance, 0).wait_recv()

                @pl.when(z < 3)
                def _():
                    self.hop(z - distance, 0).start()

            @pl.when(z + distance <= 3)
            def _():
                self.hop(z + distance, 1).wait_recv()

                @pl.when(z > 0)
                def _():
                    self.hop(z + distance, 1).start()

        def finish(self):
            for distance in range(4):
                @pl.when((z - distance >= 0) & (z < 3))
                def _():
                    self.hop(z - distance, 0, distance == 0).wait_send()

                @pl.when((z + distance <= 3) & (z > 0))
                def _():
                    self.hop(z + distance, 1, distance == 0).wait_send()

    line_x = Line(x_ref, gx)
    line_c = Line(c_ref, gc)
    line_x.begin()

    half = pl.ds(2 * c, 2)
    e_in = [send(e_ref.at[half, turn(x, k)], eb.at[x, half], take(1), xp[k]) for k in (1, 3, 2)]
    local_e = pltpu.make_async_copy(e_ref.at[:, x], eb.at[x], ls.at[0])
    local_w = pltpu.make_async_copy(w_ref.at[:, x], wb.at[x], ls.at[1])
    local_e.start()
    local_w.start()

    wide = x_ref[...].astype(F32)
    stat_x[0] = jnp.broadcast_to(jnp.sum(wide * wide, axis=0, keepdims=True), (8, tok))
    stat_a = [send(stat_x.at[0], stat_x.at[k], take(1), xp[k]) for k in (1, 2, 3)]
    gx[z] = x_ref[...]
    gc[z] = c_ref[...]
    for copy in stat_a:
        copy.wait_recv()
    stat_z[0] = stat_x[0] + stat_x[1] + stat_x[2] + stat_x[3]
    stat_b = [send(stat_z.at[0], stat_z.at[k], take(1), zp[k]) for k in (1, 2, 3)]

    local_e.wait()

    def turn_e(block):
        for j in range(4):
            ebt[block, :, j * chunk : (j + 1) * chunk] = jnp.transpose(
                eb[block, j].astype(F32)
            ).astype(BF16)

    def turn_w(block):
        for j in range(4):
            wbt[block, :, j * sub : (j + 1) * sub] = jnp.transpose(
                wb[block, j].astype(F32)
            ).astype(BF16)

    turn_e(x)
    line_x.step(1)
    e_fwd = []
    for copy, k in zip(e_in, (1, 3, 2)):
        copy.wait_recv()
        at = turn(x, -k)
        e_fwd.append(send(eb.at[at, half], eb.at[at, half], take(1), cp))
    w_in = [send(w_ref.at[half, turn(x, k)], wb.at[x, half], take(1), xp[k]) for k in (1, 3, 2)]
    line_x.step(2)
    line_c.begin()
    for copy, k in zip(e_fwd, (1, 3, 2)):
        copy.wait_recv()
        turn_e(turn(x, -k))
    for copy in stat_b:
        copy.wait_recv()
    total = stat_z[0] + stat_z[1] + stat_z[2] + stat_z[3]
    scale = lax.rsqrt(total[0:1] * (1.0 / features) + 1e-05)
    line_x.step(3)
    for j in range(4):
        rows = slice(j * chunk, (j + 1) * chunk)
        normed[rows] = (gx[j].astype(F32) * scale * gain_ref[rows]).astype(BF16)

    def scatter(make, out, landed, to):
        copies = []
        for k in (2, 1, 3):
            out[k] = make(k).astype(BF16)
            copies.append(send(out.at[k], landed.at[k], take(1), to[k]))
        acc[...] = make(0)
        return copies

    def collect(copies, landed):
        total = acc[...]
        for copy, k in zip(copies, (2, 1, 3)):
            copy.wait_recv()
            total = total + landed[k].astype(F32)
        return total

    def share(slots, value, to):
        slots[x] = value.astype(BF16)
        return [send(slots.at[x], slots.at[x], take(1), to[k]) for k in (2, 1, 3)]

    def arrive(copies):
        for copy in copies:
            copy.wait_recv()

    r_copies = scatter(lambda k: nn(ebt[turn(x, k)], normed[...]), r_s, r_r, xp)
    line_c.step(1)
    r_all = share(r_g, collect(r_copies, r_r), xp)
    local_w.wait()
    turn_w(x)
    w_fwd = []
    for copy, k in zip(w_in, (1, 3, 2)):
        copy.wait_recv()
        at = turn(x, -k)
        w_fwd.append(send(wb.at[at, half], wb.at[at, half], take(1), cp))
    line_c.step(2)
    for copy, k in zip(w_fwd, (1, 3, 2)):
        copy.wait_recv()
        turn_w(turn(x, -k))
    arrive(r_all)

    def p_part(k):
        at = turn(z, k)
        total = nn(wb[0, at], r_g[0])
        for j in range(1, 4):
            total = total + nn(wb[j, at], r_g[j])
        return total

    p_copies = scatter(p_part, p_s, p_r, zp)
    p_sum = acc[...]
    o_own[0:sub] = p_sum
    line_c.step(3)

    def b_part(k):
        total = nn(ebt[turn(x, k), :, 0:chunk], gc[0])
        for j in range(1, 4):
            total = total + nn(ebt[turn(x, k), :, j * chunk : (j + 1) * chunk], gc[j])
        return total

    b_copies = scatter(b_part, b_s, b_r, xp)
    b_g[z] = collect(b_copies, b_r).astype(BF16)
    line_b = Line(b_g.at[z], b_g)
    line_b.begin()

    acc[...] = o_own[0:sub]
    p_all = share(p_g, collect(p_copies, p_r), xp)
    line_b.step(1)
    line_b.step(2)
    arrive(p_all)
    line_b.step(3)

    def q_part(k):
        at = turn(x, k)
        total = nn(wbt[at, :, 0:sub], b_g[0])
        for j in range(1, 4):
            total = total + nn(wbt[at, :, j * sub : (j + 1) * sub], b_g[j])
        return total

    q_copies = scatter(q_part, q_s, q_r, xp)

    def o_part(k):
        at = turn(z, k)
        total = nn(eb[0, at], p_g[0])
        for j in range(1, 4):
            total = total + nn(eb[j, at], p_g[j])
        return total

    q_all = share(q_g, collect(q_copies, q_r), xp)

    o_copies = []
    for k in (2, 1, 3):
        o_s[k] = o_part(k).astype(BF16)
        o_copies.append(send(o_s.at[k], o_r.at[k], take(1), zp[k]))
    o_own[...] = o_part(0)

    order = (0, 2, 1, 3)
    for t, k in enumerate(order):
        for j in range(4):
            grad[t, j * chunk : (j + 1) * chunk] = nt(gc[j], p_g[turn(x, -k)])

    halves = 2 * chunk
    quarter, eighth = halves // 4, halves // 8
    stage = {}

    def grad_block(t):
        at = turn(x, -order[t])
        if t:
            q_all[t - 1].wait_recv()
        back = q_g[at]
        away = pl.ds(pl.multiple_of((1 - c) * halves, halves), halves)
        home = pl.ds(pl.multiple_of(c * halves, halves), halves)
        gs[t] = (grad[t, away] + nt(normed[away], back)).astype(BF16)
        stage["c", t] = send(gs.at[t], gr.at[t], take(1), cp)
        grad[t, home] = grad[t, home] + nt(normed[home], back)

    def over_y(t):
        stage["c", t].wait_recv()
        copies = []
        for k in (2, 1, 3, 0):
            at = turn(y, k) * quarter
            mine = pl.ds(pl.multiple_of(c * halves + at, quarter), quarter)
            theirs = pl.ds(pl.multiple_of(at, quarter), quarter)
            total = grad[t, mine] + gr[t, theirs].astype(F32)
            if k:
                ys[t, k] = total.astype(BF16)
                copies.append(send(ys.at[t, k], yr.at[t, k], take(1), yp[k]))
            else:
                y_own[t] = total
        stage["y", t] = copies

    def over_h(t):
        arrive(stage["y", t])
        def part(at):
            rows = pl.ds(pl.multiple_of(at * eighth, eighth), eighth)
            total = y_own[t, rows]
            for k in (1, 2, 3):
                total = total + yr[t, k, rows].astype(F32)
            return total
        zs[t] = part(1 - h).astype(BF16)
        stage["h", t] = send(zs.at[t], zr.at[t], take(1), hp)
        z_own[t] = part(h)

    piece = c * 8 + y * 2 + h

    def over_x(t):
        stage["h", t].wait_recv()
        total = (z_own[t] + zr[t].astype(F32)).astype(BF16)
        k = order[t]
        if k:
            x_s[t] = total
            stage["x", t] = send(x_s.at[t], fg.at[piece, x], take(1), xp[(4 - k) % 4])
        else:
            fg[piece, x] = total

    grad_block(0)
    grad_block(1)
    over_y(0)
    grad_block(2)
    over_y(1)
    over_h(0)
    grad_block(3)
    over_y(2)
    over_h(1)
    over_x(0)
    over_y(3)
    over_h(2)
    over_x(1)
    over_h(3)
    over_x(2)
    over_x(3)

    total = x_ref[...].astype(F32) + o_own[...]
    for copy, k in zip(o_copies, (2, 1, 3)):
        copy.wait_recv()
        total = total + o_r[k].astype(F32)
    mixed_ref[...] = total.astype(BF16)

    for t in (1, 2, 3):
        stage["x", t].wait_recv()

    def give(at, to):
        return send(fg.at[at], fg.at[at], take(1), to)

    from_h = give(piece, hp)
    from_y0 = [give(piece, yp[k]) for k in (2, 1, 3)]
    from_c = [give(piece, cp)]
    from_h.wait_recv()
    other = c * 8 + y * 2 + (1 - h)
    from_y1 = [give(other, yp[k]) for k in (2, 1, 3)]
    from_c.append(give(other, cp))
    for copies, at_h in ((from_y0, h), (from_y1, 1 - h)):
        for copy, k in zip(copies, (2, 1, 3)):
            copy.wait_recv()
            from_c.append(give(c * 8 + turn(y, -k) * 2 + at_h, cp))
    arrive(from_c)

    line_x.finish()
    line_c.finish()
    line_b.finish()
    for copy in pending:
        copy.wait_send()


def per_device(tokens, norm_gain, expansion, small_weight, cotangent):
    tok, chunk = tokens.shape
    sub = expansion.shape[1]
    x = lax.axis_index("fsdp") % 4
    gain = lax.dynamic_index_in_dim(norm_gain.reshape(4, 4, chunk), x, 1, False)
    gain = gain.reshape(4 * chunk, 1)
    half, eighth = 2 * chunk, chunk // 4
    quarter = half // 4

    def v(*shape, dtype=BF16):
        return pltpu.VMEM(shape, dtype)

    trio = [v(4, sub, tok)] * 3
    mixed, pieces = pl.pallas_call(
        kernel,
        out_shape=[
            jax.ShapeDtypeStruct((chunk, tok), BF16),
            jax.ShapeDtypeStruct((16, 4, eighth, sub), BF16),
        ],
        in_specs=[
            pl.BlockSpec(memory_space=pltpu.VMEM),
            pl.BlockSpec(memory_space=pltpu.VMEM),
            pl.BlockSpec(memory_space=pl.ANY),
            pl.BlockSpec(memory_space=pl.ANY),
            pl.BlockSpec(memory_space=pltpu.VMEM),
        ],
        out_specs=[pl.BlockSpec(memory_space=pltpu.VMEM)] * 2,
        scratch_shapes=[
            v(4, 8, tok, dtype=F32), v(4, 8, tok, dtype=F32),
            v(4, chunk, tok), v(4, chunk, tok), v(4 * chunk, tok),
            v(4, 4, chunk, sub), v(4, sub, 4 * chunk),
            v(4, 4, sub, sub), v(4, sub, 4 * sub),
            *trio, *trio, *trio, *trio,
            v(4, chunk, tok), v(4, chunk, tok), v(sub, tok, dtype=F32), v(chunk, tok, dtype=F32),
            v(4, 4 * chunk, sub, dtype=F32),
            v(4, half, sub), v(4, half, sub),
            v(4, 4, quarter, sub), v(4, 4, quarter, sub),
            v(4, eighth, sub), v(4, eighth, sub),
            v(4, quarter, sub, dtype=F32), v(4, eighth, sub, dtype=F32), v(4, eighth, sub),
            pltpu.SemaphoreType.DMA((N_SEMS,)),
            pltpu.SemaphoreType.DMA((N_SEMS,)),
            pltpu.SemaphoreType.DMA((2,)),
        ],
        compiler_params=pltpu.CompilerParams(
            collective_id=0, has_side_effects=True, vmem_limit_bytes=60 * 1024 * 1024
        ),
        name="width_growth",
    )(
        tokens.T,
        gain,
        expansion.reshape(4, 4, chunk, sub),
        small_weight.reshape(4, 4, sub, sub),
        cotangent.T,
    )
    grad = pieces.reshape(4, 4, 4, eighth, sub).transpose(0, 2, 1, 3, 4)
    return mixed.T, grad.reshape(16 * chunk, sub).astype(F32)


def solution(mesh):
    in_specs = (P("dp", "fsdp"), P(), P(None, "fsdp"), P(None, "fsdp"), P("dp", "fsdp"))
    out_specs = (P("dp", "fsdp"), P(None, "fsdp"))
    return jax.shard_map(
        per_device, mesh=mesh, in_specs=in_specs, out_specs=out_specs, check_vma=False
    )
```

time: 789 us -> 195 us (0.25)
  waiting for transfers between devices: 720 us -> 0 us
  Pallas kernels: 0 us -> 186 us
  matrix products: 41.5 us -> 0 us
  between operations: 14.1 us -> 0.68 us
    psum x1 -> x0, waiting for transfers between devices: 250 us -> none  [per_device(): grad = lax.psum(grad, 'dp')]
    all_gather x3 -> x0, waiting for transfers between devices: 246 us -> none  [the longest x1 87.2 us: per_device(): lax.all_gather(cotangent, 'fsdp', axis=1, tiled=True)]
    reduce_scatter x2 -> x0, waiting for transfers between devices: 223 us -> none  [the longest x1 123 us: per_device(): lax.psum_scatter(partial_out, 'fsdp', scatter_dimension=1, tiled=True)]
    pallas_call x0 -> x1, Pallas kernels: none -> 186 us  [per_device(): pl.pallas_call(kernel, out_shape=[jax.ShapeDtypeStruct((chunk, tok), BF16...]
    dot_general x5 -> x0, matrix products: 41.5 us -> none  [the longest x2 19.7 us: transpose_dot(): lax.dot_general(left, right, (((0,), (0,)), ((), ())), preferred_element_...]
  transfers between devices with their start and end apart: 6 -> 0, of which waited for: 6 -> 0; matrix products, arithmetic and copies ran while one was open for 5% -> 0% of each run, Pallas kernels for 0% -> 0%
where the time goes in v1:
time: 195 us
  Pallas kernels  186 us (95%)
  local copies, waits for them, and re-layouts  5.63 us (3%)
  other arithmetic  2.42 us (1%)
    pallas_call x1, Pallas kernels, per_device(): pl.pallas_call(kernel, out_shape=[jax.ShapeDtypeStruct((chunk, tok), BF16...  186 us

profile of v1, /device:TPU:1, one launch (start us, length us, event | category | flops | bytes accessed | tf_op | source)
XLA Modules:
  0.0 195.0 jit_solution(9136813101284398800)
XLA Ops:
  0.6 0.8 reshape.23
  1.5 1.4 reshape.29.gain_ref
  2.9 186.2 %width_growth.1 = (bf16[320,512]{1,0:T(8,128)(2,1)}, bf16[16,4,80,256]{3,2,1,0:T(8,128)(2,1)}) custom-call(bf16[320,512]{1,0:T(8,128)(2,1)} %bitcast.14, f32[1280,1]{1,0:T(8,128)} %reshape.29.gain_ref, bf16[4,4,320,256]{3,2,1,0:T(8,128)(2,1)} %bitcast.11, bf16[4,4,256,256]{3,2,1,0:T(8,128)(2,1)} %bitcast.13, bf16[320,512]{1,0:T(8,128)(2,1)} %bitcast.15), custom_call_target="tpu_custom_call" | custom-call | tf_op jit(solution)/shard_map/width_growth/pallas_call | solution.py:394
  189.1 2.4 %convert_bitcast_fusion = f32[4,4,4,80,256]{4,3,1,2,0:T(8,128)S(1)} fusion(bf16[4,4,4,80,256]{4,3,2,1,0:T(8,128)(2,1)} %bitcast.12), kind=kLoop, calls=%fused_computation | loop fusion | flops 1310720 | bytes 7864320 | tf_op jit(solution)/shard_map/convert_element_type | solution.py:436
  191.5 0.0 copy-start
  191.6 2.7 %copy.9 = f32[4,4,4,80,256]{4,3,2,1,0:T(8,128)} copy(f32[4,4,4,80,256]{4,3,1,2,0:T(8,128)S(1)} %convert_bitcast_fusion) | data formatting | bytes 10485760 | tf_op jit(solution)/shard_map/convert_element_type | solution.py:436
  194.3 0.0 copy-done
  194.3 0.7 copy.11
  (1 shorter events, 0.0 us)
Async XLA Ops:
  191.5 2.7 %copy-start = (bf16[320,512]{1,0:T(8,128)(2,1)S(1)}, bf16[320,512]{1,0:T(8,128)(2,1)}, u32[]{:S(2)}) copy-start(bf16[320,512]{1,0:T(8,128)(2,1)} %get-tuple-element.4) | copy-start | bytes 983044

commit v2 on v1

v2 whole, which is shorter than its diff:
```python
import jax
import jax.numpy as jnp
from jax import lax
from jax.experimental import pallas as pl
from jax.experimental.pallas import tpu as pltpu
from jax.sharding import PartitionSpec as P

MESH = pl.DeviceIdType.MESH
F32 = jnp.float32
BF16 = jnp.bfloat16
N_SEMS = 192
HALVES = 2


def nn(a, b):
    return lax.dot_general(a, b, (((1,), (0,)), ((), ())), preferred_element_type=F32)


def nt(a, b):
    return lax.dot_general(a, b, (((1,), (1,)), ((), ())), preferred_element_type=F32)


def kernel(
    x_ref, gain_ref, e_ref, w_ref, c_ref, mixed_ref, fg,
    stat_x, stat_z, gain, gx, gc, normed, eb, ebt, wb, wbt,
    r_s, r_r, r_g, p_s, p_r, p_g, b_s, b_r, b_g, q_s, q_r, q_g,
    o_s, o_r, own, o_own, grad, gs, gr, ys, yr, zs, zr, y_own, z_own, x_s,
    ss, rs, ls,
):
    chunk, tok = x_ref.shape
    part = tok // HALVES
    sub = w_ref.shape[2]
    features = chunk * 16
    d, f = lax.axis_index("dp"), lax.axis_index("fsdp")
    y, h, c = d // 4, (d // 2) % 2, d % 2
    z, x = f // 4, f % 4

    def dev(y=y, h=h, c=c, z=z, x=x):
        return {"dp": y * 4 + h * 2 + c, "fsdp": z * 4 + x}

    def turn(v, k):
        return lax.rem(v + k + 4, 4)

    xp = [dev(x=turn(x, k)) for k in range(4)]
    zp = [dev(z=turn(z, k)) for k in range(4)]
    yp = [dev(y=turn(y, k)) for k in range(4)]
    hp, cp = dev(h=1 - h), dev(c=1 - c)

    barrier = pltpu.get_barrier_semaphore()
    friends = xp[1:] + zp[1:] + yp[1:] + [hp, cp]
    for friend in friends:
        pl.semaphore_signal(barrier, inc=1, device_id=friend, device_id_type=MESH)
    pl.semaphore_wait(barrier, len(friends))

    counter = [0]
    pending = []
    lines = []

    def take(n):
        at = counter[0]
        counter[0] += n
        assert counter[0] <= N_SEMS
        return at

    def remote(src, dst, send_sem, recv_sem, to):
        return pltpu.make_async_remote_copy(
            src_ref=src, dst_ref=dst, send_sem=ss.at[send_sem], recv_sem=rs.at[recv_sem],
            device_id=to, device_id_type=MESH,
        )

    def send(src, dst, to):
        sem = take(1)
        copy = remote(src, dst, sem, sem, to)
        copy.start()
        pending.append(copy)
        return copy

    def arrive(copies):
        for copy in copies:
            copy.wait_recv()

    class Line:
        def __init__(self, own, slots):
            self.own, self.slots, self.sem = own, slots, take(5)
            lines.append(self)

        def sends(self):
            for way, (ok, to) in enumerate((
                (z < 3, z + 1), (z > 0, z - 1), (z < 2, z + 2), (z > 1, z - 2),
            )):
                to = jnp.clip(to, 0, 3)
                yield ok, remote(
                    self.own, self.slots.at[z], self.sem + way, self.sem + z, dev(z=to)
                )

        def handed(self):
            at = jnp.clip(3 * (2 - z), 0, 3)
            to = jnp.clip(3 * (z - 1), 0, 3)
            return at, remote(
                self.slots.at[at], self.slots.at[at], self.sem + 4, self.sem + at, dev(z=to)
            )

        def begin(self):
            for ok, copy in self.sends():
                @pl.when(ok)
                def _():
                    copy.start()

        def hand_over(self):
            @pl.when((z == 1) | (z == 2))
            def _():
                at, copy = self.handed()
                copy.wait_recv()
                copy.start()

        def arrive(self):
            for s in range(4):
                ok = z != s
                if s == 0:
                    ok = ok & (z != 2)
                if s == 3:
                    ok = ok & (z != 1)

                @pl.when(ok)
                def _():
                    block = self.slots.at[s]
                    remote(block, block, self.sem, self.sem + s, dev(z=turn(z, 1))).wait_recv()

        def finish(self):
            for ok, copy in self.sends():
                @pl.when(ok)
                def _():
                    copy.wait_send()

            @pl.when((z == 1) | (z == 2))
            def _():
                self.handed()[1].wait_send()

    both = range(HALVES)

    def cut(ref, i):
        return ref.at[:, pl.ds(i * part, part)]

    line_x = [Line(cut(x_ref, i), gx.at[i]) for i in both]
    line_c = [Line(cut(c_ref, i), gc.at[i]) for i in both]
    line_x[0].begin()

    half = pl.ds(2 * c, 2)
    e_in = [send(e_ref.at[half, turn(x, k)], eb.at[x, half], xp[k]) for k in (1, 3, 2)]
    local_e = pltpu.make_async_copy(e_ref.at[:, x], eb.at[x], ls.at[0])
    local_w = pltpu.make_async_copy(w_ref.at[:, x], wb.at[x], ls.at[1])
    local_e.start()
    local_w.start()

    wide = x_ref[...].astype(F32)
    stat_x[0] = jnp.broadcast_to(jnp.sum(wide * wide, axis=0, keepdims=True), (8, tok))
    stat_a = [send(stat_x.at[0], stat_x.at[k], xp[k]) for k in (1, 2, 3)]
    for i in both[1:]:
        line_x[i].begin()
    for i in both:
        gx[i, z] = x_ref[:, i * part : (i + 1) * part]
        gc[i, z] = c_ref[:, i * part : (i + 1) * part]
    rows = lax.broadcasted_iota(jnp.int32, (chunk, chunk), 0)
    cols = lax.broadcasted_iota(jnp.int32, (chunk, chunk), 1)
    for j in range(4):
        line = gain_ref[pl.ds(j * 4 + x, 1)]
        gain[j] = jnp.sum(jnp.where(rows == cols, line, 0.0), axis=1, keepdims=True)
    arrive(stat_a)
    stat_z[0] = stat_x[0] + stat_x[1] + stat_x[2] + stat_x[3]
    stat_b = [send(stat_z.at[0], stat_z.at[k], zp[k]) for k in (1, 2, 3)]

    def turn_e(block):
        ebt[block] = jnp.transpose(eb[block].reshape(4 * chunk, sub))

    def turn_w(block):
        wbt[block] = jnp.transpose(wb[block].reshape(4 * sub, sub))

    local_e.wait()
    turn_e(x)
    line_x[0].hand_over()
    e_fwd = []
    for copy, k in zip(e_in, (1, 3, 2)):
        copy.wait_recv()
        at = turn(x, -k)
        e_fwd.append(send(eb.at[at, half], eb.at[at, half], cp))
    w_in = [send(w_ref.at[half, turn(x, k)], wb.at[x, half], xp[k]) for k in (1, 3, 2)]
    line_x[0].arrive()
    line_c[0].begin()
    arrive(stat_b)
    total = stat_z[0] + stat_z[1] + stat_z[2] + stat_z[3]
    scale = lax.rsqrt(total[0:1] * (1.0 / features) + 1e-05)

    def norm(i):
        for j in range(4):
            wide = gx[i, j].astype(F32) * scale[:, i * part : (i + 1) * part] * gain[j]
            normed[i, j * chunk : (j + 1) * chunk] = wide.astype(BF16)

    norm(0)
    for copy, k in zip(e_fwd, (1, 3, 2)):
        copy.wait_recv()
        turn_e(turn(x, -k))

    def scatter(make, out, landed, mine, to):
        copies = []
        for k in (2, 1, 3):
            out[k] = make(k).astype(BF16)
            copies.append(send(out.at[k], landed.at[k], to[k]))
        mine[...] = make(0)
        return copies

    def collect(copies, landed, mine):
        total = mine[...]
        for copy, k in zip(copies, (2, 1, 3)):
            copy.wait_recv()
            total = total + landed[k].astype(F32)
        return total

    def share(slots, value):
        slots[x] = value.astype(BF16)
        return [send(slots.at[x], slots.at[x], xp[k]) for k in (2, 1, 3)]

    def stacked(block):
        return block.reshape(block.shape[0] * block.shape[1], block.shape[2])

    def scatter_r(i):
        return scatter(
            lambda k: nn(ebt[turn(x, k)], normed[i]), r_s.at[i], r_r.at[i], own.at[0, i], xp
        )

    def scatter_p(i):
        def make(k):
            at = turn(z, k)
            total = nn(wb[0, at], r_g[i, 0])
            for j in range(1, 4):
                total = total + nn(wb[j, at], r_g[i, j])
            return total

        return scatter(make, p_s.at[i], p_r.at[i], own.at[1, i], zp)

    def scatter_b(i):
        return scatter(
            lambda k: nn(ebt[turn(x, k)], stacked(gc[i])),
            b_s.at[i], b_r.at[i], own.at[2, i], xp,
        )

    def scatter_q(i):
        return scatter(
            lambda k: nn(wbt[turn(x, k)], stacked(b_g[i])),
            q_s.at[i], q_r.at[i], own.at[3, i], xp,
        )

    def scatter_o(i):
        def make(k):
            at = turn(z, k)
            total = nn(eb[0, at], p_g[i, 0])
            for j in range(1, 4):
                total = total + nn(eb[j, at], p_g[i, j])
            return total

        return scatter(make, o_s.at[i], o_r.at[i], o_own.at[i], zp)

    r_sum, r_all, p_sum, p_all = {}, {}, {}, {}
    b_sum, q_sum, q_all, o_sum = {}, {}, {}, {}
    r_sum[0] = scatter_r(0)
    line_x[1].hand_over()
    line_x[1].arrive()
    line_c[1].begin()
    norm(1)
    r_sum[1] = scatter_r(1)
    line_c[0].hand_over()
    r_all[0] = share(r_g.at[0], collect(r_sum[0], r_r.at[0], own.at[0, 0]))
    local_w.wait()
    w_fwd = []
    for copy, k in zip(w_in, (1, 3, 2)):
        copy.wait_recv()
        at = turn(x, -k)
        w_fwd.append(send(wb.at[at, half], wb.at[at, half], cp))
    r_all[1] = share(r_g.at[1], collect(r_sum[1], r_r.at[1], own.at[0, 1]))
    line_c[0].arrive()
    arrive(w_fwd)

    arrive(r_all[0])
    p_sum[0] = scatter_p(0)
    b_sum[0] = scatter_b(0)
    line_c[1].hand_over()
    arrive(r_all[1])
    p_sum[1] = scatter_p(1)
    line_c[1].arrive()
    b_sum[1] = scatter_b(1)

    line_b = [Line(b_g.at[i, z], b_g.at[i]) for i in both]

    def gather_b(i):
        b_g[i, z] = collect(b_sum[i], b_r.at[i], own.at[2, i]).astype(BF16)
        line_b[i].begin()

    gather_b(0)
    p_all[0] = share(p_g.at[0], collect(p_sum[0], p_r.at[0], own.at[1, 0]))
    line_b[0].hand_over()
    gather_b(1)
    p_all[1] = share(p_g.at[1], collect(p_sum[1], p_r.at[1], own.at[1, 1]))
    for j in range(4):
        turn_w(j)

    line_b[0].arrive()
    q_sum[0] = scatter_q(0)
    line_b[1].hand_over()
    arrive(p_all[0])
    order = (0, 2, 1, 3)

    def cotangent_part(i, t):
        at = turn(x, -order[t])
        for j in range(4):
            rows = slice(j * chunk, (j + 1) * chunk)
            product = nt(gc[i, j], p_g[i, at])
            grad[t, rows] = product if i == 0 else grad[t, rows] + product

    line_b[1].arrive()
    q_sum[1] = scatter_q(1)
    q_all[0] = share(q_g.at[0], collect(q_sum[0], q_r.at[0], own.at[3, 0]))
    o_sum[0] = scatter_o(0)
    arrive(p_all[1])
    q_all[1] = share(q_g.at[1], collect(q_sum[1], q_r.at[1], own.at[3, 1]))
    o_sum[1] = scatter_o(1)
    for t in range(4):
        for i in both:
            cotangent_part(i, t)

    halves = 2 * chunk
    quarter, eighth = halves // 4, halves // 8
    stage = {}

    def grad_block(t):
        at = turn(x, -order[t])
        if t:
            for i in both:
                q_all[i][t - 1].wait_recv()
        away = pl.ds(pl.multiple_of((1 - c) * halves, halves), halves)
        home = pl.ds(pl.multiple_of(c * halves, halves), halves)

        def total(rows):
            value = grad[t, rows]
            for i in both:
                value = value + nt(normed[i, rows], q_g[i, at])
            return value

        gs[t] = total(away).astype(BF16)
        stage["c", t] = send(gs.at[t], gr.at[t], cp)
        grad[t, home] = total(home)

    def over_y(t):
        stage["c", t].wait_recv()
        copies = []
        for k in (2, 1, 3, 0):
            at = turn(y, k) * quarter
            mine = pl.ds(pl.multiple_of(c * halves + at, quarter), quarter)
            theirs = pl.ds(pl.multiple_of(at, quarter), quarter)
            total = grad[t, mine] + gr[t, theirs].astype(F32)
            if k:
                ys[t, k] = total.astype(BF16)
                copies.append(send(ys.at[t, k], yr.at[t, k], yp[k]))
            else:
                y_own[t] = total
        stage["y", t] = copies

    def over_h(t):
        arrive(stage["y", t])

        def share_of(at):
            rows = pl.ds(pl.multiple_of(at * eighth, eighth), eighth)
            total = y_own[t, rows]
            for k in (1, 2, 3):
                total = total + yr[t, k, rows].astype(F32)
            return total

        zs[t] = share_of(1 - h).astype(BF16)
        stage["h", t] = send(zs.at[t], zr.at[t], hp)
        z_own[t] = share_of(h)

    def piece(c, y, h):
        return c * 2 + y // 2, (y % 2) * 2 + h

    first, last = piece(c, y, h)

    def over_x(t):
        stage["h", t].wait_recv()
        total = (z_own[t] + zr[t].astype(F32)).astype(BF16)
        k = order[t]
        if k:
            x_s[t] = total
            stage["x", t] = send(x_s.at[t], fg.at[first, x, last], xp[(4 - k) % 4])
        else:
            fg[first, x, last] = total

    grad_block(0)
    grad_block(1)
    over_y(0)
    grad_block(2)
    over_y(1)
    over_h(0)
    grad_block(3)
    over_y(2)
    over_h(1)
    over_x(0)
    over_y(3)
    over_h(2)
    over_x(1)
    over_h(3)
    over_x(2)
    over_x(3)

    for t in (1, 2, 3):
        stage["x", t].wait_recv()

    def give(at, to):
        return send(fg.at[at[0], :, at[1]], fg.at[at[0], :, at[1]], to)

    from_h = give(piece(c, y, h), hp)
    from_y0 = [give(piece(c, y, h), yp[k]) for k in (2, 1, 3)]
    from_c = [give(piece(c, y, h), cp)]
    from_h.wait_recv()
    from_y1 = [give(piece(c, y, 1 - h), yp[k]) for k in (2, 1, 3)]
    from_c.append(give(piece(c, y, 1 - h), cp))
    for copies, at_h in ((from_y0, h), (from_y1, 1 - h)):
        for copy, k in zip(copies, (2, 1, 3)):
            copy.wait_recv()
            from_c.append(give(piece(c, turn(y, -k), at_h), cp))

    for i in both:
        total = x_ref[:, i * part : (i + 1) * part].astype(F32)
        mixed_ref[:, i * part : (i + 1) * part] = (
            total + collect(o_sum[i], o_r.at[i], o_own.at[i])
        ).astype(BF16)
    arrive(from_c)

    for line in lines:
        line.finish()
    for copy in pending:
        copy.wait_send()


def per_device(tokens, norm_gain, expansion, small_weight, cotangent):
    tok, chunk = tokens.shape
    sub = expansion.shape[1]
    half, eighth = 2 * chunk, chunk // 4
    quarter, part = half // 4, tok // HALVES

    def v(*shape, dtype=BF16):
        return pltpu.VMEM(shape, dtype)

    trio = [v(HALVES, 4, sub, part)] * 3
    mixed, pieces = pl.pallas_call(
        kernel,
        out_shape=[
            jax.ShapeDtypeStruct((chunk, tok), BF16),
            jax.ShapeDtypeStruct((4, 4, 4, eighth, sub), BF16),
        ],
        in_specs=[
            pl.BlockSpec(memory_space=pltpu.VMEM),
            pl.BlockSpec(memory_space=pltpu.VMEM),
            pl.BlockSpec(memory_space=pl.ANY),
            pl.BlockSpec(memory_space=pl.ANY),
            pl.BlockSpec(memory_space=pltpu.VMEM),
        ],
        out_specs=[pl.BlockSpec(memory_space=pltpu.VMEM)] * 2,
        scratch_shapes=[
            v(4, 8, tok, dtype=F32), v(4, 8, tok, dtype=F32), v(4, chunk, 1, dtype=F32),
            v(HALVES, 4, chunk, part), v(HALVES, 4, chunk, part), v(HALVES, 4 * chunk, part),
            v(4, 4, chunk, sub), v(4, sub, 4 * chunk),
            v(4, 4, sub, sub), v(4, sub, 4 * sub),
            *trio, *trio, *trio, *trio,
            v(HALVES, 4, chunk, part), v(HALVES, 4, chunk, part),
            v(4, HALVES, sub, part, dtype=F32), v(HALVES, chunk, part, dtype=F32),
            v(4, 4 * chunk, sub, dtype=F32),
            v(4, half, sub), v(4, half, sub),
            v(4, 4, quarter, sub), v(4, 4, quarter, sub),
            v(4, eighth, sub), v(4, eighth, sub),
            v(4, quarter, sub, dtype=F32), v(4, eighth, sub, dtype=F32), v(4, eighth, sub),
            pltpu.SemaphoreType.DMA((N_SEMS,)),
            pltpu.SemaphoreType.DMA((N_SEMS,)),
            pltpu.SemaphoreType.DMA((2,)),
        ],
        compiler_params=pltpu.CompilerParams(
            collective_id=0, has_side_effects=True, vmem_limit_bytes=60 * 1024 * 1024
        ),
        name="width_growth",
    )(
        tokens.T,
        norm_gain.reshape(16, chunk),
        expansion.reshape(4, 4, chunk, sub),
        small_weight.reshape(4, 4, sub, sub),
        cotangent.T,
    )
    return mixed.T, pieces.reshape(16 * chunk, sub).astype(F32)


def solution(mesh):
    in_specs = (P("dp", "fsdp"), P(), P(None, "fsdp"), P(None, "fsdp"), P("dp", "fsdp"))
    out_specs = (P("dp", "fsdp"), P(None, "fsdp"))
    return jax.shard_map(
        per_device, mesh=mesh, in_specs=in_specs, out_specs=out_specs, check_vma=False
    )
```

time: 195 us -> 173 us (0.89)
  Pallas kernels: 186 us -> 166 us
  local copies, waits for them, and re-layouts: 5.63 us -> 2.14 us
  other arithmetic: 2.42 us -> 4.56 us
    pallas_call x1, Pallas kernels: 186 us -> 166 us  [per_device(): pl.pallas_call(kernel, out_shape=[jax.ShapeDtypeStruct((chunk, tok), BF16...]
    convert_element_type x1 -> x0, local copies, waits for them, and re-layouts: 2.7 us -> none  [per_device(): return (mixed.T, grad.reshape(16 * chunk, sub).astype(F32))]
    convert_element_type x1, other arithmetic: 2.42 us -> 4.56 us  [per_device(): return (mixed.T, pieces.reshape(16 * chunk, sub).astype(F32))]
where the time goes in v2:
time: 173 us
  Pallas kernels  166 us (96%)
  other arithmetic  4.56 us (3%)
  local copies, waits for them, and re-layouts  2.14 us (1%)
    pallas_call x1, Pallas kernels, per_device(): pl.pallas_call(kernel, out_shape=[jax.ShapeDtypeStruct((chunk, tok), BF16...  166 us
    convert_element_type x1, other arithmetic, per_device(): return (mixed.T, pieces.reshape(16 * chunk, sub).astype(F32))  4.56 us

profile of v2, /device:TPU:1, one launch (start us, length us, event | category | flops | bytes accessed | tf_op | source)
XLA Modules:
  0.0 173.1 jit_solution(10301450921308094613)
XLA Ops:
  0.6 1.4 reshape.16.gain_ref
  2.0 165.7 %width_growth.1 = (bf16[320,512]{1,0:T(8,128)(2,1)}, bf16[4,4,4,80,256]{4,3,2,1,0:T(8,128)(2,1)}) custom-call(bf16[320,512]{1,0:T(8,128)(2,1)} %bitcast.11, f32[16,320]{1,0:T(8,128)} %reshape.16.gain_ref, bf16[4,4,320,256]{3,2,1,0:T(8,128)(2,1)} %bitcast.8, bf16[4,4,256,256]{3,2,1,0:T(8,128)(2,1)} %bitcast.9, bf16[320,512]{1,0:T(8,128)(2,1)} %bitcast.12), custom_call_target="tpu_custom_call" | custom-call | tf_op jit(solution)/shard_map/width_growth/pallas_call | solution.py:452
  167.8 0.0 copy-start
  167.8 4.6 %bitcast_convert_fusion = f32[5120,256]{1,0:T(8,128)} fusion(bf16[4,4,4,80,256]{4,3,2,1,0:T(8,128)(2,1)} %get-tuple-element.5), kind=kLoop, calls=%fused_computation | loop fusion | flops 1310720 | bytes 7864320 | tf_op jit(solution)/shard_map/convert_element_type | solution.py:494
  172.3 0.0 copy-done
  172.3 0.7 copy.8
Async XLA Ops:
  167.8 4.6 %copy-start = (bf16[320,512]{1,0:T(8,128)(2,1)S(1)}, bf16[320,512]{1,0:T(8,128)(2,1)}, u32[]{:S(2)}) copy-start(bf16[320,512]{1,0:T(8,128)(2,1)} %get-tuple-element.4) | copy-start | bytes 983044

commit v3 on v2

--- a/solution.py
+++ b/solution.py
@@ -8,7 +8,7 @@
 MESH = pl.DeviceIdType.MESH
 F32 = jnp.float32
 BF16 = jnp.bfloat16
-N_SEMS = 192
+N_SEMS = 256
 HALVES = 2
 
 
@@ -24,7 +24,7 @@
     x_ref, gain_ref, e_ref, w_ref, c_ref, mixed_ref, fg,
     stat_x, stat_z, gain, gx, gc, normed, eb, ebt, wb, wbt,
     r_s, r_r, r_g, p_s, p_r, p_g, b_s, b_r, b_g, q_s, q_r, q_g,
-    o_s, o_r, own, o_own, grad, gs, gr, ys, yr, zs, zr, y_own, z_own, x_s,
+    o_s, o_r, p_h, o_h, own, o_own, grad, gs, gr, ys, yr, zs, zr, y_own, z_own, x_s,
     ss, rs, ls,
 ):
     chunk, tok = x_ref.shape
@@ -47,7 +47,8 @@
     hp, cp = dev(h=1 - h), dev(c=1 - c)
 
     barrier = pltpu.get_barrier_semaphore()
-    friends = xp[1:] + zp[1:] + yp[1:] + [hp, cp]
+    xhp = [dev(x=turn(x, k), h=1 - h) for k in range(4)]
+    friends = xp[1:] + zp[1:] + yp[1:] + xhp + [cp]
     for friend in friends:
         pl.semaphore_signal(barrier, inc=1, device_id=friend, device_id_type=MESH)
     pl.semaphore_wait(barrier, len(friends))
@@ -135,6 +136,63 @@
             @pl.when((z == 1) | (z == 2))
             def _():
                 self.handed()[1].wait_send()
+
+    class LineSum:
+        def __init__(self, make, out, landed, held, mine):
+            self.out, self.landed, self.held, self.mine = out, landed, held, mine
+            self.sem = take(5)
+            lines.append(self)
+            for k in (3, 1):
+                out[k] = make(turn(z, k)).astype(BF16)
+                self.copy(k).start()
+            held[...] = make(turn(z, 2))
+
+            @pl.when((z == 0) | (z == 3))
+            def _():
+                out[2] = held[...].astype(BF16)
+                self.copy(2).start()
+
+            mine[...] = make(z)
+
+        def copy(self, k):
+            if k == 3:
+                to, slot = jnp.where(z > 0, z - 1, 1), jnp.where(z > 0, z, 4)
+            elif k == 1:
+                to, slot = jnp.where(z < 3, z + 1, 2), jnp.where(z < 3, z, 4)
+            else:
+                to, slot = turn(z, 2), z
+            return remote(
+                self.out.at[k], self.landed.at[slot], self.sem + k, self.sem + slot, dev(z=to)
+            )
+
+        def landing(self, s):
+            block = self.landed.at[s]
+            return remote(block, block, self.sem, self.sem + s, dev(z=turn(z, 1)))
+
+        def hand_over(self):
+            @pl.when((z == 1) | (z == 2))
+            def _():
+                self.landing(4).wait_recv()
+                total = self.held[...] + self.landed[4].astype(F32)
+                self.out[2] = total.astype(BF16)
+                self.copy(2).start()
+
+        def collect(self):
+            for s in range(4):
+                ok = z != s
+                if s in (0, 3):
+                    ok = ok & (z != 3 - s)
+
+                @pl.when(ok)
+                def _():
+                    self.landing(s).wait_recv()
+                    self.mine[...] = self.mine[...] + self.landed[s].astype(F32)
+
+            return self.mine[...]
+
+        def finish(self):
+            for k in (1, 2, 3):
+                self.copy(k).wait_send()
 
     both = range(HALVES)
 
@@ -196,6 +254,7 @@
             normed[i, j * chunk : (j + 1) * chunk] = wide.astype(BF16)
 
     norm(0)
+    line_x[1].hand_over()
     for copy, k in zip(e_fwd, (1, 3, 2)):
         copy.wait_recv()
         turn_e(turn(x, -k))
@@ -228,14 +287,13 @@
         )
 
     def scatter_p(i):
-        def make(k):
-            at = turn(z, k)
+        def make(at):
             total = nn(wb[0, at], r_g[i, 0])
             for j in range(1, 4):
                 total = total + nn(wb[j, at], r_g[i, j])
             return total
 
-        return scatter(make, p_s.at[i], p_r.at[i], own.at[1, i], zp)
+        return LineSum(make, p_s.at[i], p_r.at[i], p_h.at[i], own.at[1, i])
 
     def scatter_b(i):
         return scatter(
@@ -250,19 +308,17 @@
         )
 
     def scatter_o(i):
-        def make(k):
-            at = turn(z, k)
+        def make(at):
             total = nn(eb[0, at], p_g[i, 0])
             for j in range(1, 4):
                 total = total + nn(eb[j, at], p_g[i, j])
             return total
 
-        return scatter(make, o_s.at[i], o_r.at[i], o_own.at[i], zp)
+        return LineSum(make, o_s.at[i], o_r.at[i], o_h.at[i], o_own.at[i])
 
     r_sum, r_all, p_sum, p_all = {}, {}, {}, {}
     b_sum, q_sum, q_all, o_sum = {}, {}, {}, {}
     r_sum[0] = scatter_r(0)
-    line_x[1].hand_over()
     line_x[1].arrive()
     line_c[1].begin()
     norm(1)
@@ -281,8 +337,9 @@
 
     arrive(r_all[0])
     p_sum[0] = scatter_p(0)
+    line_c[1].hand_over()
     b_sum[0] = scatter_b(0)
-    line_c[1].hand_over()
+    p_sum[0].hand_over()
     arrive(r_all[1])
     p_sum[1] = scatter_p(1)
     line_c[1].arrive()
@@ -295,10 +352,11 @@
         line_b[i].begin()
 
     gather_b(0)
-    p_all[0] = share(p_g.at[0], collect(p_sum[0], p_r.at[0], own.at[1, 0]))
+    p_sum[1].hand_over()
+    p_all[0] = share(p_g.at[0], p_sum[0].collect())
     line_b[0].hand_over()
     gather_b(1)
-    p_all[1] = share(p_g.at[1], collect(p_sum[1], p_r.at[1], own.at[1, 1]))
+    p_all[1] = share(p_g.at[1], p_sum[1].collect())
     for j in range(4):
         turn_w(j)
 
@@ -315,16 +373,15 @@
             product = nt(gc[i, j], p_g[i, at])
             grad[t, rows] = product if i == 0 else grad[t, rows] + product
 
+    o_sum[0] = scatter_o(0)
     line_b[1].arrive()
     q_sum[1] = scatter_q(1)
+    arrive(p_all[1])
+    o_sum[1] = scatter_o(1)
     q_all[0] = share(q_g.at[0], collect(q_sum[0], q_r.at[0], own.at[3, 0]))
-    o_sum[0] = scatter_o(0)
-    arrive(p_all[1])
+    for i in both:
+        cotangent_part(i, 0)
     q_all[1] = share(q_g.at[1], collect(q_sum[1], q_r.at[1], own.at[3, 1]))
-    o_sum[1] = scatter_o(1)
-    for t in range(4):
-        for i in both:
-            cotangent_part(i, t)
 
     halves = 2 * chunk
     quarter, eighth = halves // 4, halves // 8
@@ -389,48 +446,85 @@
         if k:
             x_s[t] = total
             stage["x", t] = send(x_s.at[t], fg.at[first, x, last], xp[(4 - k) % 4])
+            stage["xh", t] = send(x_s.at[t], fg.at[first, x, last], xhp[(4 - k) % 4])
         else:
             fg[first, x, last] = total
+            slot = fg.at[first, x, last]
+            stage["xh", t] = send(slot, slot, hp)
+
+    given = {}
+
+    def give(t, at, to):
+        block = turn(x, order[t])
+        return send(fg.at[at[0], block, at[1]], fg.at[at[0], block, at[1]], to)
+
+    from_c = []
+
+    def out_own(t):
+        if t:
+            stage["x", t].wait_recv()
+        at = piece(c, y, h)
+        given["y", t, 0] = [give(t, at, yp[k]) for k in (2, 1, 3)]
+        from_c.append(give(t, at, cp))
+
+    def out_other(t):
+        stage["xh", t].wait_recv()
+        at = piece(c, y, 1 - h)
+        given["y", t, 1] = [give(t, at, yp[k]) for k in (2, 1, 3)]
+        from_c.append(give(t, at, cp))
+
+    def out_core(t, other):
+        for copy, k in zip(given["y", t, other], (2, 1, 3)):
+            copy.wait_recv()
+            from_c.append(give(t, piece(c, turn(y, -k), 1 - h if other else h), cp))
+
+    def finish_mixed():
+        for i in both:
+            total = x_ref[:, i * part : (i + 1) * part].astype(F32)
+            mixed_ref[:, i * part : (i + 1) * part] = (
+                total + o_sum[i].collect()
+            ).astype(BF16)
 
     grad_block(0)
+    o_sum[0].hand_over()
+    over_y(0)
+    for t in (1, 2):
+        for i in both:
+            cotangent_part(i, t)
     grad_block(1)
-    over_y(0)
+    o_sum[1].hand_over()
+    over_h(0)
+    for i in both:
+        cotangent_part(i, 3)
     grad_block(2)
     over_y(1)
-    over_h(0)
     grad_block(3)
     over_y(2)
+    over_x(0)
+    out_own(0)
     over_h(1)
-    over_x(0)
     over_y(3)
     over_h(2)
     over_x(1)
+    out_other(0)
     over_h(3)
     over_x(2)
+    out_own(1)
+    out_core(0, 0)
     over_x(3)
-
-    for t in (1, 2, 3):
-        stage["x", t].wait_recv()
-
-    def give(at, to):
-        return send(fg.at[at[0], :, at[1]], fg.at[at[0], :, at[1]], to)
-
-    from_h = give(piece(c, y, h), hp)
-    from_y0 = [give(piece(c, y, h), yp[k]) for k in (2, 1, 3)]
-    from_c = [give(piece(c, y, h), cp)]
-    from_h.wait_recv()
-    from_y1 = [give(piece(c, y, 1 - h), yp[k]) for k in (2, 1, 3)]
-    from_c.append(give(piece(c, y, 1 - h), cp))
-    for copies, at_h in ((from_y0, h), (from_y1, 1 - h)):
-        for copy, k in zip(copies, (2, 1, 3)):
-            copy.wait_recv()
-            from_c.append(give(piece(c, turn(y, -k), at_h), cp))
-
-    for i in both:
-        total = x_ref[:, i * part : (i + 1) * part].astype(F32)
-        mixed_ref[:, i * part : (i + 1) * part] = (
-            total + collect(o_sum[i], o_r.at[i], o_own.at[i])
-        ).astype(BF16)
+    out_own(2)
+    out_other(1)
+    out_core(0, 1)
+    out_own(3)
+    out_core(1, 0)
+    out_other(2)
+    out_core(1, 1)
+    out_core(2, 0)
+    out_other(3)
+    finish_mixed()
+    out_core(2, 1)
+    out_core(3, 0)
+    out_core(3, 1)
     arrive(from_c)
 
     for line in lines:
@@ -449,6 +543,7 @@
         return pltpu.VMEM(shape, dtype)
 
     trio = [v(HALVES, 4, sub, part)] * 3
+    line_trio = [v(HALVES, 4, sub, part), v(HALVES, 5, sub, part), v(HALVES, 4, sub, part)]
     mixed, pieces = pl.pallas_call(
         kernel,
         out_shape=[
@@ -468,8 +563,9 @@
             v(HALVES, 4, chunk, part), v(HALVES, 4, chunk, part), v(HALVES, 4 * chunk, part),
             v(4, 4, chunk, sub), v(4, sub, 4 * chunk),
             v(4, 4, sub, sub), v(4, sub, 4 * sub),
-            *trio, *trio, *trio, *trio,
-            v(HALVES, 4, chunk, part), v(HALVES, 4, chunk, part),
+            *trio, *line_trio, *trio, *trio,
+            v(HALVES, 4, chunk, part), v(HALVES, 5, chunk, part),
+            v(HALVES, sub, part, dtype=F32), v(HALVES, chunk, part, dtype=F32),
             v(4, HALVES, sub, part, dtype=F32), v(HALVES, chunk, part, dtype=F32),
             v(4, 4 * chunk, sub, dtype=F32),
             v(4, half, sub), v(4, half, sub),

time: 173 us -> 170 us (0.983)
  Pallas kernels: 166 us -> 162 us
    pallas_call x1, Pallas kernels: 166 us -> 162 us  [per_device(): pl.pallas_call(kernel, out_shape=[jax.ShapeDtypeStruct((chunk, tok), BF16...]
where the time goes in v3:
time: 170 us; the launch traced here: 169 us
  Pallas kernels  162 us (95%)
  other arithmetic  4.56 us (3%)
  local copies, waits for them, and re-layouts  2.14 us (1%)
    pallas_call x1, Pallas kernels, per_device(): pl.pallas_call(kernel, out_shape=[jax.ShapeDtypeStruct((chunk, tok), BF16...  162 us
    convert_element_type x1, other arithmetic, per_device(): return (mixed.T, pieces.reshape(16 * chunk, sub).astype(F32))  4.56 us

profile of v3, /device:TPU:1, one launch (start us, length us, event | category | flops | bytes accessed | tf_op | source)
XLA Modules:
  0.0 169.4 jit_solution(16116469356097470112)
XLA Ops:
  0.6 1.4 reshape.16.gain_ref
  2.0 162.1 %width_growth.1 = (bf16[320,512]{1,0:T(8,128)(2,1)}, bf16[4,4,4,80,256]{4,3,2,1,0:T(8,128)(2,1)}) custom-call(bf16[320,512]{1,0:T(8,128)(2,1)} %bitcast.11, f32[16,320]{1,0:T(8,128)} %reshape.16.gain_ref, bf16[4,4,320,256]{3,2,1,0:T(8,128)(2,1)} %bitcast.8, bf16[4,4,256,256]{3,2,1,0:T(8,128)(2,1)} %bitcast.9, bf16[320,512]{1,0:T(8,128)(2,1)} %bitcast.12), custom_call_target="tpu_custom_call" | custom-call | tf_op jit(solution)/shard_map/width_growth/pallas_call | solution.py:547
  164.1 0.0 copy-start
  164.1 4.6 %bitcast_convert_fusion = f32[5120,256]{1,0:T(8,128)} fusion(bf16[4,4,4,80,256]{4,3,2,1,0:T(8,128)(2,1)} %get-tuple-element.5), kind=kLoop, calls=%fused_computation | loop fusion | flops 1310720 | bytes 7864320 | tf_op jit(solution)/shard_map/convert_element_type | solution.py:590
  168.7 0.0 copy-done
  168.7 0.7 copy.8
Async XLA Ops:
  164.1 4.6 %copy-start = (bf16[320,512]{1,0:T(8,128)(2,1)S(1)}, bf16[320,512]{1,0:T(8,128)(2,1)}, u32[]{:S(2)}) copy-start(bf16[320,512]{1,0:T(8,128)(2,1)} %get-tuple-element.4) | copy-start | bytes 983044

commit v4 on v3

--- a/solution.py
+++ b/solution.py
@@ -221,7 +221,9 @@
     rows = lax.broadcasted_iota(jnp.int32, (chunk, chunk), 0)
     cols = lax.broadcasted_iota(jnp.int32, (chunk, chunk), 1)
     for j in range(4):
-        line = gain_ref[pl.ds(j * 4 + x, 1)]
+        at = (j * 2 + x // 2) * 5 + (x % 2) * 2
+        line = jnp.concatenate([gain_ref[pl.ds(at + n, 1)] for n in range(3)], axis=1)
+        line = jnp.where(x % 2 == 0, line[:, :chunk], line[:, 64 : 64 + chunk])
         gain[j] = jnp.sum(jnp.where(rows == cols, line, 0.0), axis=1, keepdims=True)
     arrive(stat_a)
     stat_z[0] = stat_x[0] + stat_x[1] + stat_x[2] + stat_x[3]
@@ -488,17 +490,15 @@
     grad_block(0)
     o_sum[0].hand_over()
     over_y(0)
-    for t in (1, 2):
+    for t in (1, 2, 3):
         for i in both:
             cotangent_part(i, t)
     grad_block(1)
     o_sum[1].hand_over()
-    over_h(0)
-    for i in both:
-        cotangent_part(i, 3)
     grad_block(2)
     over_y(1)
     grad_block(3)
+    over_h(0)
     over_y(2)
     over_x(0)
     out_own(0)
@@ -582,7 +582,7 @@
         name="width_growth",
     )(
         tokens.T,
-        norm_gain.reshape(16, chunk),
+        norm_gain.reshape(chunk // 8, 128),
         expansion.reshape(4, 4, chunk, sub),
         small_weight.reshape(4, 4, sub, sub),
         cotangent.T,

time: 170 us -> 168 us (0.988)
  no operation moved by 1% of the time
where the time goes in v4:
time: 168 us; the launch traced here: 167 us
  Pallas kernels  161 us (96%)
  other arithmetic  4.56 us (3%)
    pallas_call x1, Pallas kernels, per_device(): pl.pallas_call(kernel, out_shape=[jax.ShapeDtypeStruct((chunk, tok), BF16...  161 us
    convert_element_type x1, other arithmetic, per_device(): return (mixed.T, pieces.reshape(16 * chunk, sub).astype(F32))  4.56 us

profile of v4, /device:TPU:1, one launch (start us, length us, event | category | flops | bytes accessed | tf_op | source)
XLA Modules:
  0.0 167.3 jit_solution(4768639424950184003)
XLA Ops:
  0.6 161.3 %width_growth.1 = (bf16[320,512]{1,0:T(8,128)(2,1)}, bf16[4,4,4,80,256]{4,3,2,1,0:T(8,128)(2,1)}) custom-call(bf16[320,512]{1,0:T(8,128)(2,1)} %bitcast.11, f32[40,128]{1,0:T(8,128)} %bitcast.14, bf16[4,4,320,256]{3,2,1,0:T(8,128)(2,1)} %bitcast.9, bf16[4,4,256,256]{3,2,1,0:T(8,128)(2,1)} %bitcast.10, bf16[320,512]{1,0:T(8,128)(2,1)} %bitcast.12), custom_call_target="tpu_custom_call" | custom-call | tf_op jit(solution)/shard_map/width_growth/pallas_call | solution.py:547
  162.0 0.0 copy-start
  162.0 4.6 %bitcast_convert_fusion = f32[5120,256]{1,0:T(8,128)} fusion(bf16[4,4,4,80,256]{4,3,2,1,0:T(8,128)(2,1)} %get-tuple-element.5), kind=kLoop, calls=%fused_computation | loop fusion | flops 1310720 | bytes 7864320 | tf_op jit(solution)/shard_map/convert_element_type | solution.py:590
  166.5 0.0 copy-done
  166.5 0.7 copy.8
Async XLA Ops:
  162.0 4.6 %copy-start = (bf16[320,512]{1,0:T(8,128)(2,1)S(1)}, bf16[320,512]{1,0:T(8,128)(2,1)}, u32[]{:S(2)}) copy-start(bf16[320,512]{1,0:T(8,128)(2,1)} %get-tuple-element.4) | copy-start | bytes 983044

commit v5 on v4

--- a/solution.py
+++ b/solution.py
@@ -238,6 +238,7 @@
     local_e.wait()
     turn_e(x)
     line_x[0].hand_over()
+    line_c[0].begin()
     e_fwd = []
     for copy, k in zip(e_in, (1, 3, 2)):
         copy.wait_recv()
@@ -245,7 +246,6 @@
         e_fwd.append(send(eb.at[at, half], eb.at[at, half], cp))
     w_in = [send(w_ref.at[half, turn(x, k)], wb.at[x, half], xp[k]) for k in (1, 3, 2)]
     line_x[0].arrive()
-    line_c[0].begin()
     arrive(stat_b)
     total = stat_z[0] + stat_z[1] + stat_z[2] + stat_z[3]
     scale = lax.rsqrt(total[0:1] * (1.0 / features) + 1e-05)
@@ -376,13 +376,14 @@
             grad[t, rows] = product if i == 0 else grad[t, rows] + product
 
     o_sum[0] = scatter_o(0)
+    for t in range(4):
+        cotangent_part(0, t)
     line_b[1].arrive()
     q_sum[1] = scatter_q(1)
+    q_all[0] = share(q_g.at[0], collect(q_sum[0], q_r.at[0], own.at[3, 0]))
     arrive(p_all[1])
+    cotangent_part(1, 0)
     o_sum[1] = scatter_o(1)
-    q_all[0] = share(q_g.at[0], collect(q_sum[0], q_r.at[0], own.at[3, 0]))
-    for i in both:
-        cotangent_part(i, 0)
     q_all[1] = share(q_g.at[1], collect(q_sum[1], q_r.at[1], own.at[3, 1]))
 
     halves = 2 * chunk
@@ -491,8 +492,7 @@
     o_sum[0].hand_over()
     over_y(0)
     for t in (1, 2, 3):
-        for i in both:
-            cotangent_part(i, t)
+        cotangent_part(1, t)
     grad_block(1)
     o_sum[1].hand_over()
     grad_block(2)
@@ -501,17 +501,17 @@
     over_h(0)
     over_y(2)
     over_x(0)
-    out_own(0)
     over_h(1)
     over_y(3)
+    out_own(0)
     over_h(2)
     over_x(1)
     out_other(0)
     over_h(3)
     over_x(2)
     out_own(1)
+    over_x(3)
     out_core(0, 0)
-    over_x(3)
     out_own(2)
     out_other(1)
     out_core(0, 1)

time: 168 us -> 166 us (0.988)
  no operation moved by 1% of the time
where the time goes in v5:
time: 166 us
  Pallas kernels  160 us (96%)
  other arithmetic  4.56 us (3%)
    pallas_call x1, Pallas kernels, per_device(): pl.pallas_call(kernel, out_shape=[jax.ShapeDtypeStruct((chunk, tok), BF16...  160 us
    convert_element_type x1, other arithmetic, per_device(): return (mixed.T, pieces.reshape(16 * chunk, sub).astype(F32))  4.56 us

profile of v5, /device:TPU:1, one launch (start us, length us, event | category | flops | bytes accessed | tf_op | source)
XLA Modules:
  0.0 166.0 jit_solution(9493702721896661044)
XLA Ops:
  0.6 160.1 %width_growth.1 = (bf16[320,512]{1,0:T(8,128)(2,1)}, bf16[4,4,4,80,256]{4,3,2,1,0:T(8,128)(2,1)}) custom-call(bf16[320,512]{1,0:T(8,128)(2,1)} %bitcast.11, f32[40,128]{1,0:T(8,128)} %bitcast.14, bf16[4,4,320,256]{3,2,1,0:T(8,128)(2,1)} %bitcast.9, bf16[4,4,256,256]{3,2,1,0:T(8,128)(2,1)} %bitcast.10, bf16[320,512]{1,0:T(8,128)(2,1)} %bitcast.12), custom_call_target="tpu_custom_call" | custom-call | tf_op jit(solution)/shard_map/width_growth/pallas_call | solution.py:547
  160.7 0.0 copy-start
  160.8 4.6 %bitcast_convert_fusion = f32[5120,256]{1,0:T(8,128)} fusion(bf16[4,4,4,80,256]{4,3,2,1,0:T(8,128)(2,1)} %get-tuple-element.5), kind=kLoop, calls=%fused_computation | loop fusion | flops 1310720 | bytes 7864320 | tf_op jit(solution)/shard_map/convert_element_type | solution.py:590
  165.3 0.0 copy-done
  165.3 0.7 copy.8
Async XLA Ops:
  160.7 4.6 %copy-start = (bf16[320,512]{1,0:T(8,128)(2,1)S(1)}, bf16[320,512]{1,0:T(8,128)(2,1)}, u32[]{:S(2)}) copy-start(bf16[320,512]{1,0:T(8,128)(2,1)} %get-tuple-element.4) | copy-start | bytes 983044
